TPU v7x, 256 devices: a whole 4x4x8 slice. The times are simulated.
256 devices in a mesh: row: 16 (over z, x_hi), col: 16 (over x_lo, y, core).
Axes of the slice: x: 4 (x_hi: 2, x_lo: 2; x = x_hi * 2 + x_lo), y: 4, z: 8, core: 2. Of those that a mesh axis runs over, the one named last changes fastest.
Arguments:
- pair: bfloat16 [768, 768, 128], P('row', 'col'), may hold values from -1000 to 1000, as said below
- ln_gain: float32 [128], replicated, may hold values from 0.25 to 1.75
- w_proj: bfloat16 [128, 512], replicated, may hold values from -0.5 to 0.5
- w_gate: bfloat16 [128, 128], replicated, may hold values from -0.5 to 0.5
- out_gain: float32 [128], replicated, may hold values from 0.25 to 1.75
- w_out: bfloat16 [128, 128], replicated, may hold values from -0.5 to 0.5
Outputs:
- update: bfloat16 [768, 768, 128], P('row', 'col')
Inputs may be any that keep to these rules, and one draw needn't show every extreme that they name: `pair`: finite values.
All inputs are finite; a program needn't handle non-finite values.
Results may differ from a plain program's by a relative error of at most 0.0078.
Values may be sent and summed in bfloat16 or wider, within the bound.
A program may use at most 128 MiB of HBM per device.

v0:
```python
import jax
import jax.numpy as jnp
from jax import lax
from jax.experimental import pallas as pl
from jax.experimental.pallas import tpu as pltpu
from jax.sharding import PartitionSpec as P

epsilon = 1e-05
MESH = pl.DeviceIdType.MESH
BLK = 48
PAD = 64
HALF = 64
LAYER = 32
RING = 8
K = 768
SUB = 16
PARTS = BLK // SUB
WINDOW = 2
LATE = 2


def kernel(
    pair_hbm, ln_gain_hbm, w_proj_hbm, w_gate_hbm, out_gain_hbm, w_out_hbm, out, ring,
    pair, ln_gain, w_proj, w_gate, out_gain, w_out, normed, wide, stage, gating, w_wide, w_fold, gain,
    b_msg, a_msg, b_in, a_in, a_all, b_all, p_msg, p_in,
    load_sem, small_sem, fetch_sem, b_send, b_recv, a_send, a_recv, p_send, p_recv, ring_send, ring_recv,
):
    r, c = lax.axis_index("row"), lax.axis_index("col")
    z, xh = r // 2, r % 2
    x, y, e = xh * 2 + c // 8, (c // 2) % 4, c % 2
    me = xh * 16 + c

    def load(part):
        rows = pl.ds(part * SUB, SUB)
        return pltpu.make_async_copy(pair_hbm.at[rows], pair.at[rows], load_sem.at[part])

    smalls = [
        pltpu.make_async_copy(src, dst, small_sem.at[i])
        for i, (src, dst) in enumerate((
            (w_proj_hbm, w_proj), (ln_gain_hbm, ln_gain), (w_gate_hbm, w_gate),
            (out_gain_hbm, out_gain), (w_out_hbm, w_out),
        ))
    ]
    smalls[0].start()
    for part in range(PARTS):
        load(part).start()
    for copy in smalls[1:]:
        copy.start()

    def peer(k):
        k = k + e * (LAYER - 2 * k)
        t = (11 * k) % LAYER
        px, py, pe = (x + t // 8) % 4, (y + (t // 2) % 4) % 4, (e + t % 2) % 2
        return px // 2, (px % 2) * 8 + py * 2 + pe

    beside = (((z + 1) % RING * 2 + xh, c), ((z + RING - 1) % RING * 2 + xh, c))

    barrier = pltpu.get_barrier_semaphore()

    @pl.loop(1, LAYER)
    def _(k):
        ph, pc = peer(k)
        pl.semaphore_signal(barrier, inc=1, device_id=(2 * z + ph, pc), device_id_type=MESH)

    for way in range(2):
        pl.semaphore_signal(barrier, inc=1, device_id=beside[way], device_id_type=MESH)

    wide[:, :, 128:] = jnp.zeros((BLK, 128, 128), jnp.bfloat16)
    wide[:, PAD:, :128] = jnp.zeros((BLK, PAD, 128), jnp.bfloat16)
    wide[:, BLK:PAD, :128] = jnp.zeros((BLK, PAD - BLK, 128), jnp.bfloat16)
    for copy in smalls:
        copy.wait()

    row = lax.broadcasted_iota(jnp.int32, (128, 128), 0)
    col = lax.broadcasted_iota(jnp.int32, (128, 128), 1)
    order = (col == row % HALF * 2 + row // HALF).astype(jnp.bfloat16)
    for t in range(4):
        turned = lax.dot_general(
            order, w_proj[:, t * 128 : (t + 1) * 128], (((1,), (1,)), ((), ())), preferred_element_type=jnp.float32
        ).astype(jnp.bfloat16)
        w_wide[t // 2, t % 2 * HALF : (t % 2 + 1) * HALF, :128] = turned[:HALF]
        w_wide[t // 2, t % 2 * HALF : (t % 2 + 1) * HALF, 128:] = turned[HALF:]

    def project(which, msg, part):
        block = wide[pl.ds(part * SUB, SUB)].reshape(SUB * 128, 256)
        both = lax.dot_general(
            w_wide[which], block, (((1,), (1,)), ((), ())), preferred_element_type=jnp.float32
        )
        side = jax.nn.sigmoid(both[:HALF]) * both[HALF:]
        for j in range(SUB):
            stage[pl.ds(j, HALF, stride=SUB), :] = side[:, j * 128 : (j + 1) * 128]
        msg[part] = stage[pl.ds(0, HALF * SUB)].reshape(LAYER, 2 * SUB, 128).astype(jnp.bfloat16)

    def scatter(msg, into, send, recv, part):
        @pl.loop(1, LAYER)
        def _(k):
            ph, pc = peer(k)
            pltpu.make_async_remote_copy(
                src_ref=msg.at[part, ph * 16 + pc], dst_ref=into.at[part, me], send_sem=send, recv_sem=recv,
                device_id=(2 * z + ph, pc), device_id_type=MESH,
            ).start()

        pltpu.make_async_copy(msg.at[part, me], into.at[part, me], recv).start()

    def whole(ref, sem):
        pltpu.make_async_copy(ref, ref, sem).wait()

    for part in range(PARTS):
        load(part).wait()
        rows = pl.ds(part * SUB, SUB)
        values = pair[rows].astype(jnp.float32)
        average = jnp.mean(values, axis=-1, keepdims=True)
        centred = values - average
        spread = jnp.mean(centred * centred, axis=-1, keepdims=True)
        result = (centred * lax.rsqrt(spread + epsilon) * ln_gain[...].reshape(1, 1, 128)).astype(jnp.bfloat16)
        normed[rows] = result
        wide[rows, :BLK, :128] = result
        wide[rows, PAD : PAD + BLK, 128:] = result
        project(1, b_msg, part)
        if part == 0:
            pl.semaphore_wait(barrier, LAYER + 1)
        scatter(b_msg, b_in, b_send.at[part], b_recv.at[part], part)

    def gathered(into, part, h, ch):
        rows, lanes = slice(ch // 2 * SUB, (ch // 2 + 1) * SUB), slice(ch % 2 * PAD, ch % 2 * PAD + BLK)
        return jnp.concatenate([into[part, h * 16 + s, rows, lanes] for s in range(16)], axis=1)

    def part_of(way, part):
        return pl.ds(2 * way, 2), slice(None), pl.ds(part * SUB, SUB)

    def ring_copy(step, part, way):
        block = part_of(way, part)
        src = b_all if isinstance(step, int) and step == 0 else ring
        return pltpu.make_async_remote_copy(
            src_ref=src.at[(step, *block)], dst_ref=ring.at[(step + 1, *block)],
            send_sem=ring_send.at[way, step, part], recv_sem=ring_recv.at[way, step, part],
            device_id=beside[way], device_id_type=MESH,
        )

    def fetch(step, part, way):
        block = part_of(way, part)
        return pltpu.make_async_copy(
            ring.at[(step, *block)], b_all.at[(step, *block)], fetch_sem.at[way, step, part]
        )

    for part in range(PARTS):
        project(0, a_msg, part)

    b_all[:, :, :, BLK:, :] = jnp.zeros((RING, 4, 2, PAD - BLK, K), jnp.bfloat16)
    for part in range(PARTS):
        whole(b_in.at[part], b_recv.at[part])
        for way in range(2):
            for h in range(2):
                for ch in (2 * way, 2 * way + 1):
                    b_all[0, ch, h, part * SUB : (part + 1) * SUB, :] = gathered(b_in, part, h, ch)
            if part >= WINDOW:
                ring_copy(0, part - WINDOW, way).wait_send()
            ring_copy(0, part, way).start()

    scatter(a_msg, a_in, a_send, a_recv, slice(None))

    @pl.loop(0, PARTS)
    def _(part):
        rows = pl.ds(part * SUB, SUB)
        gate = jnp.dot(normed[rows].reshape(SUB * BLK, 128), w_gate[...], preferred_element_type=jnp.float32)
        gating[rows] = jax.nn.sigmoid(gate).reshape(SUB, BLK, 128)

    def forward(step):
        for part in range(PARTS):
            for way in range(2):
                ring_copy(step - 1, part, way).wait_recv()
                if part >= WINDOW:
                    ring_copy(step, part - WINDOW, way).wait_send()
                else:
                    ring_copy(step - 1, part - WINDOW + PARTS, way).wait_send()
                ring_copy(step, part, way).start()
                fetch(step, part, way).start()

    low = lax.broadcasted_iota(jnp.int32, (2 * BLK, 128), 1) < PAD

    def multiply(step, way):
        if not (isinstance(step, int) and step == 0):
            for part in range(PARTS):
                fetch(step, part, way).wait()
        one, two = [
            lax.dot_general(
                a_all[2 * way + i], b_all[step, 2 * way + i].reshape(2 * PAD, K),
                (((1,), (1,)), ((), ())), preferred_element_type=jnp.float32,
            )
            for i in range(2)
        ]
        first = jnp.where(low, one, pltpu.roll(two, PAD, 1)).astype(jnp.bfloat16)
        second = jnp.where(low, pltpu.roll(one, PAD, 1), two).astype(jnp.bfloat16)
        zb = (z + RING - step if way == 0 else z + step) % RING
        for je, value in ((0, first), (1, second)):
            for ih in range(2):
                p_msg[step, way, je, ih] = value[ih * BLK : (ih + 1) * BLK]
                src = p_msg.at[step, way, je, ih]
                dst = p_in.at[me * 2 + way]
                here = jnp.logical_and(ih == xh, 2 * zb + je == c)

                @pl.when(here)
                def _():
                    pltpu.make_async_copy(src, dst, p_recv).start()

                @pl.when(jnp.logical_not(here))
                def _():
                    pltpu.make_async_remote_copy(
                        src_ref=src, dst_ref=dst, send_sem=p_send, recv_sem=p_recv,
                        device_id=(2 * z + ih, 2 * zb + je), device_id_type=MESH,
                    ).start()

    for step in range(1, LATE + 1):
        forward(step)

    whole(a_in, a_recv)
    for part in range(PARTS):
        for ch in range(4):
            for h in range(2):
                a_all[ch, h * BLK + part * SUB : h * BLK + (part + 1) * SUB, :] = gathered(a_in, part, h, ch)

    for way in range(2):
        multiply(0, way)

    @pl.loop(1, LATE + 1)
    def _(step):
        for way in range(2):
            multiply(step, way)

    @pl.loop(LATE + 1, RING - 1)
    def _(step):
        forward(step)
        for way in range(2):
            multiply(step, way)

    for way in range(2):
        for part in range(PARTS):
            ring_copy(RING - 2, part, way).wait_recv()
            fetch(RING - 1, part, way).start()
    for way in range(2):
        multiply(RING - 1, way)

    for part in range(PARTS):
        whole(b_msg.at[part, pl.ds(0, LAYER - 1)], b_send.at[part])
    whole(a_msg.at[:, pl.ds(0, LAYER - 1)], a_send)
    for way in range(2):
        for part in range(PARTS - WINDOW, PARTS):
            ring_copy(RING - 2, part, way).wait_send()
    whole(p_in.at[pl.ds(0, 2 * (LAYER - 1))], p_send)
    whole(p_in, p_recv)

    folded = lax.dot_general(order, w_out[...], (((1,), (0,)), ((), ())), preferred_element_type=jnp.float32)
    w_fold[...] = folded.astype(jnp.bfloat16)
    pairs = lax.broadcasted_iota(jnp.int32, (HALF, 128), 0)
    lanes = lax.broadcasted_iota(jnp.int32, (HALF, 128), 1)
    under = lanes < PAD
    picked = [
        jnp.sum(jnp.where(lanes == 2 * pairs + i, out_gain[...], 0.0), axis=1, keepdims=True) for i in range(2)
    ]
    gain[...] = jnp.where(under, picked[0], picked[1])

    @pl.loop(0, PARTS)
    def _(part):
        rows = pl.ds(part * SUB, SUB)
        total = jnp.sum(p_in[:, rows, :].astype(jnp.float32), axis=0)
        average = (total + pltpu.roll(total, PAD, 1)) * (1.0 / 128)
        total = jnp.zeros((SUB, 128), jnp.float32)
        for s in range(HALF):
            centred = p_in[s, rows, :].astype(jnp.float32) - average
            total = total + centred * centred
        spread = (total + pltpu.roll(total, PAD, 1)) * (1.0 / 128)
        factor = lax.rsqrt(spread + epsilon)
        for s in range(HALF):
            centred = p_in[s, rows, :].astype(jnp.float32) - average
            stage[pl.ds(part * SUB + s * BLK, SUB), :] = centred * factor * gain[s : s + 1, :]

    @pl.loop(0, 6)
    def _(n):
        blocks = []
        for i in range(4):
            one = stage[pl.ds(8 * n + 2 * i, HALF, stride=BLK), :]
            two = stage[pl.ds(8 * n + 2 * i + 1, HALF, stride=BLK), :]
            even = jnp.where(under, one, pltpu.roll(two, PAD, 1))
            odd = jnp.where(under, pltpu.roll(one, PAD, 1), two)
            blocks.append(jnp.concatenate([even, odd], axis=0).astype(jnp.bfloat16))
        both = jnp.concatenate(blocks, axis=1)
        result = lax.dot_general(both, w_fold[...], (((0,), (0,)), ((), ())), preferred_element_type=jnp.float32)
        for i in range(8):
            out[8 * n + i] = (gating[8 * n + i] * result[i * PAD : i * PAD + BLK]).astype(jnp.bfloat16)


def per_device(pair, ln_gain, w_proj, w_gate, out_gain, w_out):
    bf16, f32 = jnp.bfloat16, jnp.float32
    vmem = pl.BlockSpec(memory_space=pltpu.VMEM)
    dma = pltpu.SemaphoreType.DMA
    parts = (PARTS, LAYER, 2 * SUB, 128)
    update, _ = pl.pallas_call(
        kernel,
        out_shape=(
            jax.ShapeDtypeStruct(pair.shape, bf16),
            jax.ShapeDtypeStruct((RING, 4, 2, BLK, K), bf16),
        ),
        in_specs=[pl.BlockSpec(memory_space=pl.ANY)] * 6,
        out_specs=(vmem, pl.BlockSpec(memory_space=pl.ANY)),
        scratch_shapes=[
            pltpu.VMEM((BLK, BLK, 128), bf16),
            pltpu.VMEM((1, 128), f32),
            pltpu.VMEM((128, 512), bf16),
            pltpu.VMEM((128, 128), bf16),
            pltpu.VMEM((1, 128), f32),
            pltpu.VMEM((128, 128), bf16),
            pltpu.VMEM((BLK, BLK, 128), bf16),
            pltpu.VMEM((BLK, 128, 256), bf16),
            pltpu.VMEM((HALF * BLK, 128), f32),
            pltpu.VMEM((BLK, BLK, 128), f32),
            pltpu.VMEM((2, 128, 256), bf16),
            pltpu.VMEM((128, 128), bf16),
            pltpu.VMEM((HALF, 128), f32),
            pltpu.VMEM(parts, bf16),
            pltpu.VMEM(parts, bf16),
            pltpu.VMEM(parts, bf16),
            pltpu.VMEM(parts, bf16),
            pltpu.VMEM((4, 2 * BLK, K), bf16),
            pltpu.VMEM((RING, 4, 2, PAD, K), bf16),
            pltpu.VMEM((RING, 2, 2, 2, BLK, 128), bf16),
            pltpu.VMEM((2 * LAYER, BLK, 128), bf16),
            dma((PARTS,)), dma((5,)), dma((2, RING, PARTS)),
            dma((PARTS,)), dma((PARTS,)), dma, dma,
            dma, dma,
            dma((2, RING - 1, PARTS)), dma((2, RING - 1, PARTS)),
        ],
        compiler_params=pltpu.CompilerParams(
            collective_id=0, has_side_effects=True, vmem_limit_bytes=56 * 2**20
        ),
        name="triangle",
    )(pair, ln_gain.reshape(1, 128), w_proj, w_gate, out_gain.reshape(1, 128), w_out)
    return update


def solution(mesh):
    in_specs = (P("row", "col", None), P(), P(), P(), P(), P())
    out_specs = P("row", "col", None)
    return jax.shard_map(per_device, mesh=mesh, in_specs=in_specs, out_specs=out_specs, check_vma=False)
```

profile of v0, /device:TPU:27, one launch (start us, length us, event | category | flops | bytes accessed | tf_op | source)
XLA Modules:
  0.0 79.2 jit_solution(10337316718716940983)
XLA Ops:
  0.0 77.2 %triangle.1 = (bf16[48,48,128]{2,1,0:T(8,128)(2,1)}, bf16[8,4,2,48,768]{4,3,2,1,0:T(8,128)(2,1)}) custom-call(bf16[48,48,128]{2,1,0:T(8,128)(2,1)} %pair_hbm.1, f32[1,128]{1,0:T(1,128)} %bitcast.2, bf16[128,512]{1,0:T(8,128)(2,1)} %w_proj_hbm.1, bf16[128,128]{1,0:T(8,128)(2,1)} %w_gate_hbm.1, f32[1,128]{1,0:T(1,128)} %bitcast.3, bf16[128,128]{1,0:T(8,128)(2,1)} %w_out_hbm.1), custom_call_target="tpu_custom_call" | custom-call | tf_op jit(solution)/shard_map/triangle/pallas_call | solution.py:297
  77.3 1.9 %copy.8 = bf16[48,48,128]{2,1,0:T(8,128)(2,1)} copy(bf16[48,48,128]{2,1,0:T(8,128)(2,1)} %get-tuple-element.6) | data formatting | bytes 1179648
where the time goes:
time: 79.7 us; the launch traced here: 79.2 us
  Pallas kernels  77.2 us (97%)
  local copies, waits for them, and re-layouts  1.92 us (2%)
    pallas_call x1, Pallas kernels, per_device(): pl.pallas_call(kernel, out_shape=(jax.ShapeDtypeStruct(pair.shape, bf16),...  77.2 us
    unnamed x1, local copies, waits for them, and re-layouts  1.92 us

commit v1 on v0

--- a/solution.py
+++ b/solution.py
@@ -15,15 +15,14 @@
 K = 768
 SUB = 16
 PARTS = BLK // SUB
-WINDOW = 2
-LATE = 2
+RAW = PARTS - 1
 
 
 def kernel(
-    pair_hbm, ln_gain_hbm, w_proj_hbm, w_gate_hbm, out_gain_hbm, w_out_hbm, out, ring,
+    pair_hbm, ln_gain_hbm, w_proj_hbm, w_gate_hbm, out_gain_hbm, w_out_hbm, out,
     pair, ln_gain, w_proj, w_gate, out_gain, w_out, normed, wide, stage, gating, w_wide, w_fold, gain,
-    b_msg, a_msg, b_in, a_in, a_all, b_all, p_msg, p_in,
-    load_sem, small_sem, fetch_sem, b_send, b_recv, a_send, a_recv, p_send, p_recv, ring_send, ring_recv,
+    b_msg, a_msg, b_in, a_in, raw_in, raw_all, a_all, b_all, p_msg, p_in,
+    load_sem, small_sem, b_send, b_recv, a_send, a_recv, raw_send, raw_recv, rest_send, rest_recv, p_send, p_recv, ring_send, ring_recv,
 ):
     r, c = lax.axis_index("row"), lax.axis_index("col")
     z, xh = r // 2, r % 2
@@ -91,21 +90,30 @@
             stage[pl.ds(j, HALF, stride=SUB), :] = side[:, j * 128 : (j + 1) * 128]
         msg[part] = stage[pl.ds(0, HALF * SUB)].reshape(LAYER, 2 * SUB, 128).astype(jnp.bfloat16)
 
-    def scatter(msg, into, send, recv, part):
+    def scatter(src_of, dst, send, recv):
         @pl.loop(1, LAYER)
         def _(k):
             ph, pc = peer(k)
             pltpu.make_async_remote_copy(
-                src_ref=msg.at[part, ph * 16 + pc], dst_ref=into.at[part, me], send_sem=send, recv_sem=recv,
+                src_ref=src_of(ph * 16 + pc), dst_ref=dst, send_sem=send, recv_sem=recv,
                 device_id=(2 * z + ph, pc), device_id_type=MESH,
             ).start()
 
-        pltpu.make_async_copy(msg.at[part, me], into.at[part, me], recv).start()
+        pltpu.make_async_copy(src_of(me), dst, recv).start()
+
+    def scatter_part(part):
+        scatter(lambda n: b_msg.at[part, n], b_in.at[part, me], b_send.at[part], b_recv.at[part])
+
+    def raw_copy(way):
+        return pltpu.make_async_remote_copy(
+            src_ref=b_msg.at[RAW], dst_ref=raw_in.at[way], send_sem=raw_send.at[way], recv_sem=raw_recv.at[way],
+            device_id=beside[way], device_id_type=MESH,
+        )
 
     def whole(ref, sem):
         pltpu.make_async_copy(ref, ref, sem).wait()
 
-    for part in range(PARTS):
+    for part in (RAW, 0, 1):
         load(part).wait()
         rows = pl.ds(part * SUB, SUB)
         values = pair[rows].astype(jnp.float32)
@@ -117,71 +125,52 @@
         wide[rows, :BLK, :128] = result
         wide[rows, PAD : PAD + BLK, 128:] = result
         project(1, b_msg, part)
-        if part == 0:
+        if part == RAW:
             pl.semaphore_wait(barrier, LAYER + 1)
-        scatter(b_msg, b_in, b_send.at[part], b_recv.at[part], part)
-
-    def gathered(into, part, h, ch):
+            for way in range(2):
+                raw_copy(way).start()
+        else:
+            scatter_part(part)
+    def gathered(into, h, ch):
         rows, lanes = slice(ch // 2 * SUB, (ch // 2 + 1) * SUB), slice(ch % 2 * PAD, ch % 2 * PAD + BLK)
-        return jnp.concatenate([into[part, h * 16 + s, rows, lanes] for s in range(16)], axis=1)
-
-    def part_of(way, part):
-        return pl.ds(2 * way, 2), slice(None), pl.ds(part * SUB, SUB)
+        return jnp.concatenate([into[h * 16 + s, rows, lanes] for s in range(16)], axis=1)
+
+    def gather_into(slot, way, part, into):
+        for h in range(2):
+            for ch in (2 * way, 2 * way + 1):
+                b_all[slot, ch, h, part * SUB : (part + 1) * SUB, :] = gathered(into, h, ch)
 
     def ring_copy(step, part, way):
-        block = part_of(way, part)
-        src = b_all if isinstance(step, int) and step == 0 else ring
+        block = pl.ds(2 * way, 2), slice(None), pl.ds(part * SUB, SUB)
         return pltpu.make_async_remote_copy(
-            src_ref=src.at[(step, *block)], dst_ref=ring.at[(step + 1, *block)],
+            src_ref=b_all.at[(step, *block)], dst_ref=b_all.at[(step + 1, *block)],
             send_sem=ring_send.at[way, step, part], recv_sem=ring_recv.at[way, step, part],
             device_id=beside[way], device_id_type=MESH,
         )
 
-    def fetch(step, part, way):
-        block = part_of(way, part)
-        return pltpu.make_async_copy(
-            ring.at[(step, *block)], b_all.at[(step, *block)], fetch_sem.at[way, step, part]
-        )
-
-    for part in range(PARTS):
-        project(0, a_msg, part)
-
     b_all[:, :, :, BLK:, :] = jnp.zeros((RING, 4, 2, PAD - BLK, K), jnp.bfloat16)
-    for part in range(PARTS):
+    for part in range(RAW):
         whole(b_in.at[part], b_recv.at[part])
         for way in range(2):
-            for h in range(2):
-                for ch in (2 * way, 2 * way + 1):
-                    b_all[0, ch, h, part * SUB : (part + 1) * SUB, :] = gathered(b_in, part, h, ch)
-            if part >= WINDOW:
-                ring_copy(0, part - WINDOW, way).wait_send()
+            gather_into(0, way, part, b_in.at[part])
             ring_copy(0, part, way).start()
-
-    scatter(a_msg, a_in, a_send, a_recv, slice(None))
-
-    @pl.loop(0, PARTS)
-    def _(part):
-        rows = pl.ds(part * SUB, SUB)
-        gate = jnp.dot(normed[rows].reshape(SUB * BLK, 128), w_gate[...], preferred_element_type=jnp.float32)
-        gating[rows] = jax.nn.sigmoid(gate).reshape(SUB, BLK, 128)
+    for way in range(2):
+        raw_copy(way).wait_recv()
+        scatter(lambda n: raw_in.at[way, n], raw_all.at[way, me], rest_send.at[way], rest_recv.at[way])
+
+    def sent(step):
+        return range(PARTS if 0 < step < RING - 2 else RAW)
 
     def forward(step):
-        for part in range(PARTS):
+        for part in sent(step - 1):
             for way in range(2):
                 ring_copy(step - 1, part, way).wait_recv()
-                if part >= WINDOW:
-                    ring_copy(step, part - WINDOW, way).wait_send()
-                else:
-                    ring_copy(step - 1, part - WINDOW + PARTS, way).wait_send()
-                ring_copy(step, part, way).start()
-                fetch(step, part, way).start()
+                if part in sent(step):
+                    ring_copy(step, part, way).start()
 
     low = lax.broadcasted_iota(jnp.int32, (2 * BLK, 128), 1) < PAD
 
     def multiply(step, way):
-        if not (isinstance(step, int) and step == 0):
-            for part in range(PARTS):
-                fetch(step, part, way).wait()
         one, two = [
             lax.dot_general(
                 a_all[2 * way + i], b_all[step, 2 * way + i].reshape(2 * PAD, K),
@@ -210,42 +199,59 @@
                         device_id=(2 * z + ih, 2 * zb + je), device_id_type=MESH,
                     ).start()
 
-    for step in range(1, LATE + 1):
-        forward(step)
-
+    def multiply_both(*steps):
+        for step in steps:
+            for way in range(2):
+                multiply(step, way)
+
+    forward(1)
+    scatter_part(RAW)
+    for part in range(PARTS):
+        project(0, a_msg, part)
+    scatter(lambda n: a_msg.at[:, n], a_in.at[:, me], a_send, a_recv)
+    for way in range(2):
+        whole(raw_all.at[way], rest_recv.at[way])
+        gather_into(1, way, RAW, raw_all.at[way])
+        ring_copy(1, RAW, way).start()
+        gather_into(RING - 1, 1 - way, RAW, raw_all.at[way])
+    forward(2)
+    whole(b_in.at[RAW], b_recv.at[RAW])
+    for way in range(2):
+        gather_into(0, way, RAW, b_in.at[RAW])
+
+    @pl.loop(0, PARTS)
+    def _(part):
+        rows = pl.ds(part * SUB, SUB)
+        gate = jnp.dot(normed[rows].reshape(SUB * BLK, 128), w_gate[...], preferred_element_type=jnp.float32)
+        gating[rows] = jax.nn.sigmoid(gate).reshape(SUB, BLK, 128)
+
+    forward(3)
     whole(a_in, a_recv)
     for part in range(PARTS):
         for ch in range(4):
             for h in range(2):
-                a_all[ch, h * BLK + part * SUB : h * BLK + (part + 1) * SUB, :] = gathered(a_in, part, h, ch)
-
-    for way in range(2):
-        multiply(0, way)
-
-    @pl.loop(1, LATE + 1)
-    def _(step):
-        for way in range(2):
-            multiply(step, way)
-
-    @pl.loop(LATE + 1, RING - 1)
-    def _(step):
-        forward(step)
-        for way in range(2):
-            multiply(step, way)
-
-    for way in range(2):
-        for part in range(PARTS):
+                a_all[ch, h * BLK + part * SUB : h * BLK + (part + 1) * SUB, :] = gathered(a_in.at[part], h, ch)
+    multiply_both(0, 1)
+    forward(4)
+    multiply_both(2, 3)
+    forward(5)
+    multiply_both(4, 5)
+    forward(6)
+    multiply_both(6)
+    for way in range(2):
+        for part in sent(RING - 2):
             ring_copy(RING - 2, part, way).wait_recv()
-            fetch(RING - 1, part, way).start()
-    for way in range(2):
         multiply(RING - 1, way)
 
     for part in range(PARTS):
         whole(b_msg.at[part, pl.ds(0, LAYER - 1)], b_send.at[part])
     whole(a_msg.at[:, pl.ds(0, LAYER - 1)], a_send)
     for way in range(2):
-        for part in range(PARTS - WINDOW, PARTS):
-            ring_copy(RING - 2, part, way).wait_send()
+        raw_copy(way).wait_send()
+        whole(raw_in.at[way, pl.ds(0, LAYER - 1)], rest_send.at[way])
+        for step in range(RING - 1):
+            for part in sent(step):
+                ring_copy(step, part, way).wait_send()
     whole(p_in.at[pl.ds(0, 2 * (LAYER - 1))], p_send)
     whole(p_in, p_recv)
 
@@ -294,14 +300,11 @@
     vmem = pl.BlockSpec(memory_space=pltpu.VMEM)
     dma = pltpu.SemaphoreType.DMA
     parts = (PARTS, LAYER, 2 * SUB, 128)
-    update, _ = pl.pallas_call(
+    return pl.pallas_call(
         kernel,
-        out_shape=(
-            jax.ShapeDtypeStruct(pair.shape, bf16),
-            jax.ShapeDtypeStruct((RING, 4, 2, BLK, K), bf16),
-        ),
+        out_shape=jax.ShapeDtypeStruct(pair.shape, bf16),
         in_specs=[pl.BlockSpec(memory_space=pl.ANY)] * 6,
-        out_specs=(vmem, pl.BlockSpec(memory_space=pl.ANY)),
+        out_specs=vmem,
         scratch_shapes=[
             pltpu.VMEM((BLK, BLK, 128), bf16),
             pltpu.VMEM((1, 128), f32),
@@ -320,12 +323,15 @@
             pltpu.VMEM(parts, bf16),
             pltpu.VMEM(parts, bf16),
             pltpu.VMEM(parts, bf16),
+            pltpu.VMEM((2, *parts[1:]), bf16),
+            pltpu.VMEM((2, *parts[1:]), bf16),
             pltpu.VMEM((4, 2 * BLK, K), bf16),
             pltpu.VMEM((RING, 4, 2, PAD, K), bf16),
             pltpu.VMEM((RING, 2, 2, 2, BLK, 128), bf16),
             pltpu.VMEM((2 * LAYER, BLK, 128), bf16),
-            dma((PARTS,)), dma((5,)), dma((2, RING, PARTS)),
+            dma((PARTS,)), dma((5,)),
             dma((PARTS,)), dma((PARTS,)), dma, dma,
+            dma((2,)), dma((2,)), dma((2,)), dma((2,)),
             dma, dma,
             dma((2, RING - 1, PARTS)), dma((2, RING - 1, PARTS)),
         ],
@@ -334,7 +340,6 @@
         ),
         name="triangle",
     )(pair, ln_gain.reshape(1, 128), w_proj, w_gate, out_gain.reshape(1, 128), w_out)
-    return update
 
 
 def solution(mesh):

time: 79.7 us -> 75.7 us (0.950)
  Pallas kernels: 77.2 us -> 73.6 us
    pallas_call x1, Pallas kernels: 77.2 us -> 73.6 us  [per_device(): pl.pallas_call(kernel, out_shape=jax.ShapeDtypeStruct(pair.shape, bf16),...]
where the time goes in v1:
time: 75.7 us; the launch traced here: 75.6 us
  Pallas kernels  73.6 us (97%)
  local copies, waits for them, and re-layouts  1.92 us (3%)
    pallas_call x1, Pallas kernels, per_device(): pl.pallas_call(kernel, out_shape=jax.ShapeDtypeStruct(pair.shape, bf16),...  73.6 us
    unnamed x1, local copies, waits for them, and re-layouts  1.92 us

profile of v1, /device:TPU:27, one launch (start us, length us, event | category | flops | bytes accessed | tf_op | source)
XLA Modules:
  0.0 75.6 jit_solution(5791324379849354139)
XLA Ops:
  0.0 73.6 %triangle.1 = bf16[48,48,128]{2,1,0:T(8,128)(2,1)} custom-call(bf16[48,48,128]{2,1,0:T(8,128)(2,1)} %pair_hbm.1, f32[1,128]{1,0:T(1,128)} %bitcast.2, bf16[128,512]{1,0:T(8,128)(2,1)} %w_proj_hbm.1, bf16[128,128]{1,0:T(8,128)(2,1)} %w_gate_hbm.1, f32[1,128]{1,0:T(1,128)} %bitcast.3, bf16[128,128]{1,0:T(8,128)(2,1)} %w_out_hbm.1), custom_call_target="tpu_custom_call" | custom-call | tf_op jit(solution)/shard_map/triangle/pallas_call | solution.py:303
  73.6 1.9 %copy.8 = bf16[48,48,128]{2,1,0:T(8,128)(2,1)} copy(bf16[48,48,128]{2,1,0:T(8,128)(2,1)} %triangle.1) | data formatting | bytes 1179648

commit v2 on v1

--- a/solution.py
+++ b/solution.py
@@ -21,7 +21,7 @@
 def kernel(
     pair_hbm, ln_gain_hbm, w_proj_hbm, w_gate_hbm, out_gain_hbm, w_out_hbm, out,
     pair, ln_gain, w_proj, w_gate, out_gain, w_out, normed, wide, stage, gating, w_wide, w_fold, gain,
-    b_msg, a_msg, b_in, a_in, raw_in, raw_all, a_all, b_all, p_msg, p_in,
+    b_msg, a_msg, b_in, a_in, raw_in, raw_all, a_all, b_all, p_msg, p_in, turned,
     load_sem, small_sem, b_send, b_recv, a_send, a_recv, raw_send, raw_recv, rest_send, rest_recv, p_send, p_recv, ring_send, ring_recv,
 ):
     r, c = lax.axis_index("row"), lax.axis_index("col")
@@ -74,11 +74,11 @@
     col = lax.broadcasted_iota(jnp.int32, (128, 128), 1)
     order = (col == row % HALF * 2 + row // HALF).astype(jnp.bfloat16)
     for t in range(4):
-        turned = lax.dot_general(
+        mixed = lax.dot_general(
             order, w_proj[:, t * 128 : (t + 1) * 128], (((1,), (1,)), ((), ())), preferred_element_type=jnp.float32
         ).astype(jnp.bfloat16)
-        w_wide[t // 2, t % 2 * HALF : (t % 2 + 1) * HALF, :128] = turned[:HALF]
-        w_wide[t // 2, t % 2 * HALF : (t % 2 + 1) * HALF, 128:] = turned[HALF:]
+        w_wide[t // 2, t % 2 * HALF : (t % 2 + 1) * HALF, :128] = mixed[:HALF]
+        w_wide[t // 2, t % 2 * HALF : (t % 2 + 1) * HALF, 128:] = mixed[HALF:]
 
     def project(which, msg, part):
         block = wide[pl.ds(part * SUB, SUB)].reshape(SUB * 128, 256)
@@ -148,7 +148,7 @@
             device_id=beside[way], device_id_type=MESH,
         )
 
-    b_all[:, :, :, BLK:, :] = jnp.zeros((RING, 4, 2, PAD - BLK, K), jnp.bfloat16)
+    a_all[:, :, BLK:, :] = jnp.zeros((4, 2, PAD - BLK, K), jnp.bfloat16)
     for part in range(RAW):
         whole(b_in.at[part], b_recv.at[part])
         for way in range(2):
@@ -168,34 +168,36 @@
                 if part in sent(step):
                     ring_copy(step, part, way).start()
 
-    low = lax.broadcasted_iota(jnp.int32, (2 * BLK, 128), 1) < PAD
-
-    def multiply(step, way):
+    def multiply(step, way, part=None):
+        count, begin = (BLK, 0) if part is None else (SUB, part * SUB)
+        rows = slice(begin, begin + count)
         one, two = [
             lax.dot_general(
-                a_all[2 * way + i], b_all[step, 2 * way + i].reshape(2 * PAD, K),
+                b_all[step, ch, :, rows, :].reshape(2 * count, K), a_all[ch].reshape(2 * PAD, K),
                 (((1,), (1,)), ((), ())), preferred_element_type=jnp.float32,
             )
-            for i in range(2)
+            for ch in (2 * way, 2 * way + 1)
         ]
+        low = lax.broadcasted_iota(jnp.int32, (2 * count, 128), 1) < PAD
         first = jnp.where(low, one, pltpu.roll(two, PAD, 1)).astype(jnp.bfloat16)
         second = jnp.where(low, pltpu.roll(one, PAD, 1), two).astype(jnp.bfloat16)
         zb = (z + RING - step if way == 0 else z + step) % RING
-        for je, value in ((0, first), (1, second)):
-            for ih in range(2):
-                p_msg[step, way, je, ih] = value[ih * BLK : (ih + 1) * BLK]
-                src = p_msg.at[step, way, je, ih]
-                dst = p_in.at[me * 2 + way]
+        for ih, value in ((0, first), (1, second)):
+            for je in range(2):
+                p_msg[step, way, je, ih, rows, :] = value[je * count : (je + 1) * count]
+                src = p_msg.at[step, way, je, ih, pl.ds(begin, count)]
+                dst = p_in.at[me + LAYER * way, pl.ds(begin, count)]
+                recv = p_recv.at[PARTS + way if part is None else part]
                 here = jnp.logical_and(ih == xh, 2 * zb + je == c)
 
                 @pl.when(here)
                 def _():
-                    pltpu.make_async_copy(src, dst, p_recv).start()
+                    pltpu.make_async_copy(src, dst, recv).start()
 
                 @pl.when(jnp.logical_not(here))
                 def _():
                     pltpu.make_async_remote_copy(
-                        src_ref=src, dst_ref=dst, send_sem=p_send, recv_sem=p_recv,
+                        src_ref=src, dst_ref=dst, send_sem=p_send, recv_sem=recv,
                         device_id=(2 * z + ih, 2 * zb + je), device_id_type=MESH,
                     ).start()
 
@@ -218,42 +220,6 @@
     whole(b_in.at[RAW], b_recv.at[RAW])
     for way in range(2):
         gather_into(0, way, RAW, b_in.at[RAW])
-
-    @pl.loop(0, PARTS)
-    def _(part):
-        rows = pl.ds(part * SUB, SUB)
-        gate = jnp.dot(normed[rows].reshape(SUB * BLK, 128), w_gate[...], preferred_element_type=jnp.float32)
-        gating[rows] = jax.nn.sigmoid(gate).reshape(SUB, BLK, 128)
-
-    forward(3)
-    whole(a_in, a_recv)
-    for part in range(PARTS):
-        for ch in range(4):
-            for h in range(2):
-                a_all[ch, h * BLK + part * SUB : h * BLK + (part + 1) * SUB, :] = gathered(a_in.at[part], h, ch)
-    multiply_both(0, 1)
-    forward(4)
-    multiply_both(2, 3)
-    forward(5)
-    multiply_both(4, 5)
-    forward(6)
-    multiply_both(6)
-    for way in range(2):
-        for part in sent(RING - 2):
-            ring_copy(RING - 2, part, way).wait_recv()
-        multiply(RING - 1, way)
-
-    for part in range(PARTS):
-        whole(b_msg.at[part, pl.ds(0, LAYER - 1)], b_send.at[part])
-    whole(a_msg.at[:, pl.ds(0, LAYER - 1)], a_send)
-    for way in range(2):
-        raw_copy(way).wait_send()
-        whole(raw_in.at[way, pl.ds(0, LAYER - 1)], rest_send.at[way])
-        for step in range(RING - 1):
-            for part in sent(step):
-                ring_copy(step, part, way).wait_send()
-    whole(p_in.at[pl.ds(0, 2 * (LAYER - 1))], p_send)
-    whole(p_in, p_recv)
 
     folded = lax.dot_general(order, w_out[...], (((1,), (0,)), ((), ())), preferred_element_type=jnp.float32)
     w_fold[...] = folded.astype(jnp.bfloat16)
@@ -268,31 +234,92 @@
     @pl.loop(0, PARTS)
     def _(part):
         rows = pl.ds(part * SUB, SUB)
-        total = jnp.sum(p_in[:, rows, :].astype(jnp.float32), axis=0)
+        gate = jnp.dot(normed[rows].reshape(SUB * BLK, 128), w_gate[...], preferred_element_type=jnp.float32)
+        gating[rows] = jax.nn.sigmoid(gate).reshape(SUB, BLK, 128)
+
+    forward(3)
+    whole(a_in, a_recv)
+    for part in range(PARTS):
+        for ch in range(4):
+            for h in range(2):
+                a_all[ch, h, part * SUB : (part + 1) * SUB, :] = gathered(a_in.at[part], h, ch)
+    multiply_both(0, 1)
+    forward(4)
+    multiply_both(2, 3)
+    forward(5)
+    multiply_both(4, 5)
+    forward(6)
+    multiply_both(6)
+    for way in range(2):
+        multiply(RING - 1, way, RAW)
+    for part in sent(RING - 2):
+        for way in range(2):
+            ring_copy(RING - 2, part, way).wait_recv()
+            multiply(RING - 1, way, part)
+
+    distance = (z + RING - c // 2) % RING
+    for way in range(2):
+        last = distance == (RING - 1 if way == 0 else 1)
+
+        @pl.when(jnp.logical_not(last))
+        def _():
+            whole(p_in.at[pl.ds(LAYER * way, LAYER)], p_recv.at[PARTS + way])
+
+    for part in (RAW, *sent(RING - 2)):
+        rows = pl.ds(part * SUB, SUB)
+        for way in range(2):
+            last = distance == (RING - 1 if way == 0 else 1)
+
+            @pl.when(last)
+            def _():
+                whole(p_in.at[pl.ds(LAYER * way, LAYER), rows], p_recv.at[part])
+
+        slots = [n // 2 + LAYER * (n % 2) for n in range(HALF)]
+        total = jnp.zeros((SUB, 128), jnp.float32)
+        for s in slots:
+            total = total + p_in[s, rows, :].astype(jnp.float32)
         average = (total + pltpu.roll(total, PAD, 1)) * (1.0 / 128)
         total = jnp.zeros((SUB, 128), jnp.float32)
-        for s in range(HALF):
+        for s in slots:
             centred = p_in[s, rows, :].astype(jnp.float32) - average
             total = total + centred * centred
         spread = (total + pltpu.roll(total, PAD, 1)) * (1.0 / 128)
         factor = lax.rsqrt(spread + epsilon)
-        for s in range(HALF):
+        for n, s in enumerate(slots):
             centred = p_in[s, rows, :].astype(jnp.float32) - average
-            stage[pl.ds(part * SUB + s * BLK, SUB), :] = centred * factor * gain[s : s + 1, :]
-
-    @pl.loop(0, 6)
-    def _(n):
-        blocks = []
-        for i in range(4):
-            one = stage[pl.ds(8 * n + 2 * i, HALF, stride=BLK), :]
-            two = stage[pl.ds(8 * n + 2 * i + 1, HALF, stride=BLK), :]
-            even = jnp.where(under, one, pltpu.roll(two, PAD, 1))
-            odd = jnp.where(under, pltpu.roll(one, PAD, 1), two)
-            blocks.append(jnp.concatenate([even, odd], axis=0).astype(jnp.bfloat16))
-        both = jnp.concatenate(blocks, axis=1)
-        result = lax.dot_general(both, w_fold[...], (((0,), (0,)), ((), ())), preferred_element_type=jnp.float32)
-        for i in range(8):
-            out[8 * n + i] = (gating[8 * n + i] * result[i * PAD : i * PAD + BLK]).astype(jnp.bfloat16)
+            stage[n * SUB : (n + 1) * SUB, :] = centred * factor * gain[n : n + 1, :]
+
+        for n in range(2):
+            blocks = []
+            for i in range(4):
+                one = stage[pl.ds(8 * n + 2 * i, HALF, stride=SUB), :]
+                two = stage[pl.ds(8 * n + 2 * i + 1, HALF, stride=SUB), :]
+                even = jnp.where(under, one, pltpu.roll(two, PAD, 1))
+                odd = jnp.where(under, pltpu.roll(one, PAD, 1), two)
+                blocks.append(jnp.concatenate([even, odd], axis=0).astype(jnp.bfloat16))
+            both = jnp.concatenate(blocks, axis=1)
+            result = lax.dot_general(
+                both, w_fold[...], (((0,), (0,)), ((), ())), preferred_element_type=jnp.float32
+            )
+            for j in range(8):
+                turned[pl.ds(part * SUB + 8 * n + j, BLK, stride=BLK), :] = result[j * PAD : j * PAD + BLK]
+
+    @pl.loop(0, PARTS)
+    def _(part):
+        rows = pl.ds(part * SUB, SUB)
+        result = turned[pl.ds(part * SUB * BLK, SUB * BLK), :].reshape(SUB, BLK, 128)
+        out[rows] = (gating[rows] * result).astype(jnp.bfloat16)
+
+    for part in range(PARTS):
+        whole(b_msg.at[part, pl.ds(0, LAYER - 1)], b_send.at[part])
+    whole(a_msg.at[:, pl.ds(0, LAYER - 1)], a_send)
+    whole(p_in.at[pl.ds(0, 2 * (LAYER - 1))], p_send)
+    for way in range(2):
+        raw_copy(way).wait_send()
+        whole(raw_in.at[way, pl.ds(0, LAYER - 1)], rest_send.at[way])
+        for step in range(RING - 1):
+            for part in sent(step):
+                ring_copy(step, part, way).wait_send()
 
 
 def per_device(pair, ln_gain, w_proj, w_gate, out_gain, w_out):
@@ -325,14 +352,15 @@
             pltpu.VMEM(parts, bf16),
             pltpu.VMEM((2, *parts[1:]), bf16),
             pltpu.VMEM((2, *parts[1:]), bf16),
-            pltpu.VMEM((4, 2 * BLK, K), bf16),
-            pltpu.VMEM((RING, 4, 2, PAD, K), bf16),
+            pltpu.VMEM((4, 2, PAD, K), bf16),
+            pltpu.VMEM((RING, 4, 2, BLK, K), bf16),
             pltpu.VMEM((RING, 2, 2, 2, BLK, 128), bf16),
             pltpu.VMEM((2 * LAYER, BLK, 128), bf16),
+            pltpu.VMEM((BLK * BLK, 128), f32),
             dma((PARTS,)), dma((5,)),
             dma((PARTS,)), dma((PARTS,)), dma, dma,
             dma((2,)), dma((2,)), dma((2,)), dma((2,)),
-            dma, dma,
+            dma, dma((PARTS + 2,)),
             dma((2, RING - 1, PARTS)), dma((2, RING - 1, PARTS)),
         ],
         compiler_params=pltpu.CompilerParams(

time: 75.7 us -> 72.7 us (0.960)
  Pallas kernels: 73.6 us -> 70 us
    pallas_call x1, Pallas kernels: 73.6 us -> 70 us  [per_device(): pl.pallas_call(kernel, out_shape=jax.ShapeDtypeStruct(pair.shape, bf16),...]
where the time goes in v2:
time: 72.7 us; the launch traced here: 71.9 us
  Pallas kernels  70 us (96%)
  local copies, waits for them, and re-layouts  1.92 us (3%)
    pallas_call x1, Pallas kernels, per_device(): pl.pallas_call(kernel, out_shape=jax.ShapeDtypeStruct(pair.shape, bf16),...  70 us
    unnamed x1, local copies, waits for them, and re-layouts  1.92 us

profile of v2, /device:TPU:27, one launch (start us, length us, event | category | flops | bytes accessed | tf_op | source)
XLA Modules:
  0.0 71.9 jit_solution(8919460876494669295)
XLA Ops:
  0.0 70.0 %triangle.1 = bf16[48,48,128]{2,1,0:T(8,128)(2,1)} custom-call(bf16[48,48,128]{2,1,0:T(8,128)(2,1)} %pair_hbm.1, f32[1,128]{1,0:T(1,128)} %bitcast.2, bf16[128,512]{1,0:T(8,128)(2,1)} %w_proj_hbm.1, bf16[128,128]{1,0:T(8,128)(2,1)} %w_gate_hbm.1, f32[1,128]{1,0:T(1,128)} %bitcast.3, bf16[128,128]{1,0:T(8,128)(2,1)} %w_out_hbm.1), custom_call_target="tpu_custom_call" | custom-call | tf_op jit(solution)/shard_map/triangle/pallas_call | solution.py:330
  70.0 1.9 %copy.8 = bf16[48,48,128]{2,1,0:T(8,128)(2,1)} copy(bf16[48,48,128]{2,1,0:T(8,128)(2,1)} %triangle.1) | data formatting | bytes 1179648

commit v3 on v2

--- a/solution.py
+++ b/solution.py
@@ -16,6 +16,9 @@
 SUB = 16
 PARTS = BLK // SUB
 RAW = PARTS - 1
+
+
+OFFSETS = [(2, 2, 0), (2, 2, 1), (2, 3, 0), (2, 3, 1), (3, 2, 0), (3, 2, 1), (2, 1, 0), (2, 1, 1), (1, 2, 0), (1, 2, 1), (2, 0, 0), (2, 0, 1), (0, 2, 0), (0, 2, 1), (3, 1, 0), (3, 1, 1), (1, 3, 0), (1, 3, 1), (3, 3, 0), (3, 3, 1), (1, 1, 0), (1, 1, 1), (3, 0, 0), (3, 0, 1), (0, 3, 0), (0, 3, 1), (1, 0, 0), (1, 0, 1), (0, 1, 0), (0, 1, 1), (0, 0, 1)]
 
 
 def kernel(
@@ -47,17 +50,15 @@
         copy.start()
 
     def peer(k):
-        k = k + e * (LAYER - 2 * k)
-        t = (11 * k) % LAYER
-        px, py, pe = (x + t // 8) % 4, (y + (t // 2) % 4) % 4, (e + t % 2) % 2
+        dx, dy, de = OFFSETS[k]
+        px, py, pe = (x + dx) % 4, (y + dy) % 4, (e + de) % 2
         return px // 2, (px % 2) * 8 + py * 2 + pe
 
     beside = (((z + 1) % RING * 2 + xh, c), ((z + RING - 1) % RING * 2 + xh, c))
 
     barrier = pltpu.get_barrier_semaphore()
 
-    @pl.loop(1, LAYER)
-    def _(k):
+    for k in range(LAYER - 1):
         ph, pc = peer(k)
         pl.semaphore_signal(barrier, inc=1, device_id=(2 * z + ph, pc), device_id_type=MESH)
 
@@ -91,8 +92,7 @@
         msg[part] = stage[pl.ds(0, HALF * SUB)].reshape(LAYER, 2 * SUB, 128).astype(jnp.bfloat16)
 
     def scatter(src_of, dst, send, recv):
-        @pl.loop(1, LAYER)
-        def _(k):
+        for k in range(LAYER - 1):
             ph, pc = peer(k)
             pltpu.make_async_remote_copy(
                 src_ref=src_of(ph * 16 + pc), dst_ref=dst, send_sem=send, recv_sem=recv,

time: 72.7 us -> 69.9 us (0.961)
  Pallas kernels: 70 us -> 66.9 us
    pallas_call x1, Pallas kernels: 70 us -> 66.9 us  [per_device(): pl.pallas_call(kernel, out_shape=jax.ShapeDtypeStruct(pair.shape, bf16),...]
where the time goes in v3:
time: 69.9 us; the launch traced here: 68.8 us
  Pallas kernels  66.9 us (96%)
  local copies, waits for them, and re-layouts  1.92 us (3%)
    pallas_call x1, Pallas kernels, per_device(): pl.pallas_call(kernel, out_shape=jax.ShapeDtypeStruct(pair.shape, bf16),...  66.9 us
    unnamed x1, local copies, waits for them, and re-layouts  1.92 us

profile of v3, /device:TPU:27, one launch (start us, length us, event | category | flops | bytes accessed | tf_op | source)
XLA Modules:
  0.0 68.8 jit_solution(3725609160134516815)
XLA Ops:
  0.0 66.9 %triangle.1 = bf16[48,48,128]{2,1,0:T(8,128)(2,1)} custom-call(bf16[48,48,128]{2,1,0:T(8,128)(2,1)} %pair_hbm.1, f32[1,128]{1,0:T(1,128)} %bitcast.2, bf16[128,512]{1,0:T(8,128)(2,1)} %w_proj_hbm.1, bf16[128,128]{1,0:T(8,128)(2,1)} %w_gate_hbm.1, f32[1,128]{1,0:T(1,128)} %bitcast.3, bf16[128,128]{1,0:T(8,128)(2,1)} %w_out_hbm.1), custom_call_target="tpu_custom_call" | custom-call | tf_op jit(solution)/shard_map/triangle/pallas_call | solution.py:330
  66.9 1.9 %copy.8 = bf16[48,48,128]{2,1,0:T(8,128)(2,1)} copy(bf16[48,48,128]{2,1,0:T(8,128)(2,1)} %triangle.1) | data formatting | bytes 1179648

commit v4 on v3

--- a/solution.py
+++ b/solution.py
@@ -215,8 +215,9 @@
         whole(raw_all.at[way], rest_recv.at[way])
         gather_into(1, way, RAW, raw_all.at[way])
         ring_copy(1, RAW, way).start()
+    forward(2)
+    for way in range(2):
         gather_into(RING - 1, 1 - way, RAW, raw_all.at[way])
-    forward(2)
     whole(b_in.at[RAW], b_recv.at[RAW])
     for way in range(2):
         gather_into(0, way, RAW, b_in.at[RAW])

time: 69.9 us -> 69.8 us (level)
  no operation moved by 1% of the time
where the time goes in v4:
time: 69.8 us; the launch traced here: 68.7 us
  Pallas kernels  66.7 us (96%)
  local copies, waits for them, and re-layouts  1.92 us (3%)
    pallas_call x1, Pallas kernels, per_device(): pl.pallas_call(kernel, out_shape=jax.ShapeDtypeStruct(pair.shape, bf16),...  66.7 us
    unnamed x1, local copies, waits for them, and re-layouts  1.92 us

profile of v4, /device:TPU:27, one launch (start us, length us, event | category | flops | bytes accessed | tf_op | source)
XLA Modules:
  0.0 68.7 jit_solution(4178586908200572202)
XLA Ops:
  0.0 66.7 %triangle.1 = bf16[48,48,128]{2,1,0:T(8,128)(2,1)} custom-call(bf16[48,48,128]{2,1,0:T(8,128)(2,1)} %pair_hbm.1, f32[1,128]{1,0:T(1,128)} %bitcast.2, bf16[128,512]{1,0:T(8,128)(2,1)} %w_proj_hbm.1, bf16[128,128]{1,0:T(8,128)(2,1)} %w_gate_hbm.1, f32[1,128]{1,0:T(1,128)} %bitcast.3, bf16[128,128]{1,0:T(8,128)(2,1)} %w_out_hbm.1), custom_call_target="tpu_custom_call" | custom-call | tf_op jit(solution)/shard_map/triangle/pallas_call | solution.py:331
  66.7 1.9 %copy.8 = bf16[48,48,128]{2,1,0:T(8,128)(2,1)} copy(bf16[48,48,128]{2,1,0:T(8,128)(2,1)} %triangle.1) | data formatting | bytes 1179648

commit v5 on v4

--- a/solution.py
+++ b/solution.py
@@ -222,22 +222,6 @@
     for way in range(2):
         gather_into(0, way, RAW, b_in.at[RAW])
 
-    folded = lax.dot_general(order, w_out[...], (((1,), (0,)), ((), ())), preferred_element_type=jnp.float32)
-    w_fold[...] = folded.astype(jnp.bfloat16)
-    pairs = lax.broadcasted_iota(jnp.int32, (HALF, 128), 0)
-    lanes = lax.broadcasted_iota(jnp.int32, (HALF, 128), 1)
-    under = lanes < PAD
-    picked = [
-        jnp.sum(jnp.where(lanes == 2 * pairs + i, out_gain[...], 0.0), axis=1, keepdims=True) for i in range(2)
-    ]
-    gain[...] = jnp.where(under, picked[0], picked[1])
-
-    @pl.loop(0, PARTS)
-    def _(part):
-        rows = pl.ds(part * SUB, SUB)
-        gate = jnp.dot(normed[rows].reshape(SUB * BLK, 128), w_gate[...], preferred_element_type=jnp.float32)
-        gating[rows] = jax.nn.sigmoid(gate).reshape(SUB, BLK, 128)
-
     forward(3)
     whole(a_in, a_recv)
     for part in range(PARTS):
@@ -249,6 +233,23 @@
     multiply_both(2, 3)
     forward(5)
     multiply_both(4, 5)
+
+    folded = lax.dot_general(order, w_out[...], (((1,), (0,)), ((), ())), preferred_element_type=jnp.float32)
+    w_fold[...] = folded.astype(jnp.bfloat16)
+    pairs = lax.broadcasted_iota(jnp.int32, (HALF, 128), 0)
+    lanes = lax.broadcasted_iota(jnp.int32, (HALF, 128), 1)
+    under = lanes < PAD
+    picked = [
+        jnp.sum(jnp.where(lanes == 2 * pairs + i, out_gain[...], 0.0), axis=1, keepdims=True) for i in range(2)
+    ]
+    gain[...] = jnp.where(under, picked[0], picked[1])
+
+    @pl.loop(0, PARTS)
+    def _(part):
+        rows = pl.ds(part * SUB, SUB)
+        gate = jnp.dot(normed[rows].reshape(SUB * BLK, 128), w_gate[...], preferred_element_type=jnp.float32)
+        gating[rows] = jax.nn.sigmoid(gate).reshape(SUB, BLK, 128)
+
     forward(6)
     multiply_both(6)
     for way in range(2):

time: 69.8 us -> 69.8 us (level)
  no operation moved by 1% of the time
where the time goes in v5:
time: 69.8 us; the launch traced here: 68.7 us
  Pallas kernels  66.7 us (96%)
  local copies, waits for them, and re-layouts  1.92 us (3%)
    pallas_call x1, Pallas kernels, per_device(): pl.pallas_call(kernel, out_shape=jax.ShapeDtypeStruct(pair.shape, bf16),...  66.7 us
    unnamed x1, local copies, waits for them, and re-layouts  1.92 us

profile of v5, /device:TPU:27, one launch (start us, length us, event | category | flops | bytes accessed | tf_op | source)
XLA Modules:
  0.0 68.7 jit_solution(7977898928194598130)
XLA Ops:
  0.0 66.7 %triangle.1 = bf16[48,48,128]{2,1,0:T(8,128)(2,1)} custom-call(bf16[48,48,128]{2,1,0:T(8,128)(2,1)} %pair_hbm.1, f32[1,128]{1,0:T(1,128)} %bitcast.2, bf16[128,512]{1,0:T(8,128)(2,1)} %w_proj_hbm.1, bf16[128,128]{1,0:T(8,128)(2,1)} %w_gate_hbm.1, f32[1,128]{1,0:T(1,128)} %bitcast.3, bf16[128,128]{1,0:T(8,128)(2,1)} %w_out_hbm.1), custom_call_target="tpu_custom_call" | custom-call | tf_op jit(solution)/shard_map/triangle/pallas_call | solution.py:332
  66.7 1.9 %copy.8 = bf16[48,48,128]{2,1,0:T(8,128)(2,1)} copy(bf16[48,48,128]{2,1,0:T(8,128)(2,1)} %triangle.1) | data formatting | bytes 1179648
